TPU v7x, 32 devices: a whole 2x2x4 slice. The times are simulated.
32 devices in a mesh: space: 8 (over z, x), inst: 4 (over y, core).
Axes of the slice: x: 2, y: 2, z: 4, core: 2. Of those that a mesh axis runs over, the one named last changes fastest.
Arguments:
- basis_rows: bfloat16 [2, 24576, 512], P(None, 'space'), may hold values from -0.75 to 0.75
- reference_state: float32 [2, 24576], P(None, 'space'), may hold values from -3 to 3
- burning: int32 [24576], P('space'), may hold values 0 or 1
- coords_now: float32 [4, 512], P('inst'), may hold values from -1.5 to 1.5
- coords_before: float32 [4, 512], P('inst'), may hold values from -1.5 to 1.5
- diffusivity: float32 [4], P('inst'), may hold values from 0.5 to 2
- advection: float32 [4], P('inst'), may hold values from 0.5 to 1.5
- reaction_rate: float32 [4], P('inst'), may hold values from 0.2 to 1
Outputs:
- jacobian: bfloat16 [4, 2, 24576, 512], P('inst', None, 'space')
- residual: float32 [4, 2, 24576], P('inst', None, 'space')
- update: float32 [4, 512], P('inst')
All inputs are finite; a program needn't handle non-finite values. No bound on the sum of `burning` on one device may be relied on, other than what follows from the above.
Results may differ from a plain program's by a relative error of at most 0.0034.
Values may be sent and summed in bfloat16 or wider, within the bound.
A program may use at most 128 MiB of HBM per device.

v0:
```python
import functools

import jax
import jax.numpy as jnp
from jax import lax
from jax.experimental import pallas as pl
from jax.experimental.pallas import tpu as pltpu
from jax.sharding import PartitionSpec as P

time_step = 0.5
MESH = pl.DeviceIdType.MESH
TILE = 512
ROWS = 32
LANES = 128
EDGE = 16
HIGH = lax.Precision.HIGHEST


def tn_dot(a, b, precision=None):
    return lax.dot_general(
        a, b, (((0,), (0,)), ((), ())), preferred_element_type=jnp.float32, precision=precision
    )


def nt_dot(a, b, precision=None):
    return lax.dot_general(
        a, b, (((1,), (1,)), ((), ())), preferred_element_type=jnp.float32, precision=precision
    )


def halo_kernel(n, basis, ref, low_b, high_b, low_r, high_r, send, recv):
    me = lax.axis_index("space")
    cells = basis.shape[1]
    has_low, has_high = me > 0, me < n - 1

    low_b[...] = jnp.zeros_like(low_b)
    high_b[...] = jnp.zeros_like(high_b)
    low_r[...] = jnp.zeros_like(low_r)
    high_r[...] = jnp.zeros_like(high_r)

    barrier = pltpu.get_barrier_semaphore()
    for step in (1, n - 1):
        pl.semaphore_signal(
            barrier, inc=1, device_id={"space": lax.rem(me + step, n)}, device_id_type=MESH
        )
    pl.semaphore_wait(barrier, 2)

    up = {"space": lax.rem(me + 1, n)}
    down = {"space": lax.rem(me + n - 1, n)}

    def copy(src, dst, slot, target):
        return pltpu.make_async_remote_copy(
            src_ref=src,
            dst_ref=dst,
            send_sem=send.at[slot],
            recv_sem=recv.at[slot],
            device_id=target,
            device_id_type=MESH,
        )

    to_up = [
        copy(basis.at[:, pl.ds(cells - EDGE, EDGE), :], low_b, 0, up),
        copy(ref.at[:, pl.ds(cells - LANES, LANES)], low_r, 1, up),
    ]
    to_down = [
        copy(basis.at[:, pl.ds(0, EDGE), :], high_b, 2, down),
        copy(ref.at[:, pl.ds(0, LANES)], high_r, 3, down),
    ]

    @pl.when(has_high)
    def _():
        for c in to_up:
            c.start()

    @pl.when(has_low)
    def _():
        for c in to_down:
            c.start()

    @pl.when(has_high)
    def _():
        for c in to_up:
            c.wait_send()
        for c in to_down:
            c.wait_recv()

    @pl.when(has_low)
    def _():
        for c in to_down:
            c.wait_send()
        for c in to_up:
            c.wait_recv()


def halo(n, basis, ref):
    modes = basis.shape[2]
    vmem = pl.BlockSpec(memory_space=pltpu.VMEM)
    return pl.pallas_call(
        functools.partial(halo_kernel, n),
        out_shape=[
            jax.ShapeDtypeStruct((2, EDGE, modes), jnp.bfloat16),
            jax.ShapeDtypeStruct((2, EDGE, modes), jnp.bfloat16),
            jax.ShapeDtypeStruct((2, LANES), jnp.float32),
            jax.ShapeDtypeStruct((2, LANES), jnp.float32),
        ],
        in_specs=[pl.BlockSpec(memory_space=pl.ANY)] * 2,
        out_specs=[vmem] * 4,
        scratch_shapes=[pltpu.SemaphoreType.DMA((4,)), pltpu.SemaphoreType.DMA((4,))],
        compiler_params=pltpu.CompilerParams(collective_id=0, has_side_effects=True),
    )(basis, ref)


def main_kernel(
    diffusivity, advection, rate, now_ref, before_ref, ref_ref, burn_ref, basis, before_rows,
    after_rows, low_b, high_b, low_r, high_r,
    jac, res_out, packed,
    state, coef, resid, wide, top, bottom, right,
):
    phase, tile = pl.program_id(0), pl.program_id(1)
    tiles = pl.num_programs(1)
    cells = res_out.shape[1]
    modes = basis.shape[2]
    half = modes // 2
    here = pl.ds(pl.multiple_of(tile * TILE, TILE), TILE)
    inner = pl.ds(pl.multiple_of(tile * TILE + LANES, LANES), TILE)
    h = time_step
    nu, c, k = diffusivity[0], advection[0], rate[0]

    def coords():
        now, old = now_ref[...], before_ref[...]
        row = lax.broadcasted_iota(jnp.int32, (16, modes), 0)
        both = jnp.where(row == 0, now, jnp.where(row == 1, now - old, 0.0))
        return both.astype(jnp.bfloat16)

    @pl.when(phase == 0)
    def _():
        vec = coords()

        @pl.when(tile == 0)
        def _():
            state[...] = jnp.zeros_like(state)
            resid[...] = jnp.zeros_like(resid)
            lane = lax.broadcasted_iota(jnp.int32, (1, LANES), 1)
            for v in range(2):
                low = nt_dot(vec, low_b[v])[0:1, EDGE - 1 : EDGE]
                state[v : v + 1, 0:LANES] = jnp.where(
                    lane == LANES - 1, low_r[v : v + 1, :] + low, 0.0
                )
                high = nt_dot(vec, high_b[v])[0:1, 0:1]
                state[v : v + 1, LANES + cells : 2 * LANES + cells] = jnp.where(
                    lane == 0, high_r[v : v + 1, :] + high, 0.0
                )

        for v in range(2):
            both = nt_dot(vec, basis[v])
            state[v : v + 1, inner] = both[0:1] + ref_ref[v : v + 1, here]
            state[v + 2 : v + 3, inner] = both[1:2]

    @pl.when((phase == 1) & (tile == 0))
    def _():
        top[...] = jnp.zeros_like(top)
        bottom[...] = jnp.zeros_like(bottom)
        right[...] = jnp.zeros_like(right)
        full = state[...]
        total = full.shape[1]
        centre = full[:, LANES : LANES + cells]
        left = pltpu.roll(full, 1, 1)[:, LANES : LANES + cells]
        after = pltpu.roll(full, total - 1, 1)[:, LANES : LANES + cells]
        flux = nu * (left - 2.0 * centre + after) - c * (centre - left)
        fuel, heat = centre[0:1], centre[1:2]
        active = burn_ref[...].astype(jnp.float32)
        tangent = jnp.tanh(heat)
        slope_fuel = k * active * (1.0 + tangent)
        slope_heat = k * active * fuel * (1.0 - tangent * tangent)
        reaction = k * active * fuel * (1.0 + tangent)
        res_fuel = centre[2:3] - h * (flux[0:1] - reaction)
        res_heat = centre[3:4] - h * (flux[1:2] + reaction)
        res_out[0:1, :] = res_fuel
        res_out[1:2, :] = res_heat
        resid[0:1, :] = res_fuel
        resid[1:2, :] = res_heat
        row = lax.broadcasted_iota(jnp.int32, (8, cells), 0)
        stacked = jnp.where(row == 0, h * slope_fuel, jnp.where(row == 1, h * slope_heat, 0.0))
        for part in range(cells // LANES):
            span = slice(part * LANES, (part + 1) * LANES)
            coef[span, :] = stacked[:, span].T

    @pl.when(phase == 1)
    def _():
        for v in range(2):
            wide[v, 8 : 8 + TILE, :] = basis[v].astype(jnp.float32)
            before = jnp.where(tile == 0, low_b[v], before_rows[v]).astype(jnp.float32)
            wide[v, 0:8, :] = before[EDGE - 8 : EDGE]
            after = jnp.where(tile == tiles - 1, high_b[v], after_rows[v]).astype(jnp.float32)
            wide[v, 8 + TILE : 16 + TILE, :] = after[0:8]
        base = 1.0 + 2.0 * h * nu + h * c
        to_left = -h * (nu + c)
        to_right = -h * nu

        for start in range(0, TILE, ROWS):
            at = pl.ds(pl.multiple_of(tile * TILE + start, ROWS), ROWS)
            pair = coef[at, :]
            ha, he = pair[:, 0:1], pair[:, 1:2]
            centre, side = [], []
            for v in range(2):
                centre.append(wide[v, 8 + start : 8 + start + ROWS, :])
                side.append(
                    to_left * wide[v, 7 + start : 7 + start + ROWS, :]
                    + to_right * wide[v, 9 + start : 9 + start + ROWS, :]
                )
            fuel_rows = (base + ha) * centre[0] + side[0] + he * centre[1]
            heat_rows = (base - he) * centre[1] + side[1] - ha * centre[0]
            jac[0, start : start + ROWS, :] = fuel_rows.astype(jnp.bfloat16)
            jac[1, start : start + ROWS, :] = heat_rows.astype(jnp.bfloat16)

        rows = jac[...].reshape(2 * TILE, modes)
        top[...] += tn_dot(rows[:, 0:half], rows)
        bottom[...] += tn_dot(rows[:, half:], rows[:, half:])
        both = resid[:, here].astype(jnp.bfloat16)
        part_fuel = jnp.dot(both, jac[0], preferred_element_type=jnp.float32)
        part_heat = jnp.dot(both, jac[1], preferred_element_type=jnp.float32)
        right[...] += part_fuel[0:1] + part_heat[1:2]

    @pl.when((phase == 1) & (tile == tiles - 1))
    def _():
        blocks = modes // LANES
        spot = 0
        for i in range(blocks):
            for j in range(i, blocks):
                if i * LANES < half:
                    block = top[i * LANES : (i + 1) * LANES, j * LANES : (j + 1) * LANES]
                else:
                    a, b = i * LANES - half, j * LANES - half
                    block = bottom[a : a + LANES, b : b + LANES]
                packed[spot * LANES : (spot + 1) * LANES, :] = block
                spot += 1
        used = spot * LANES
        packed[used:, :] = jnp.zeros((packed.shape[0] - used, LANES), jnp.float32)
        for i in range(blocks):
            packed[used + i : used + i + 1, :] = right[:, i * LANES : (i + 1) * LANES]


def assemble(packed_rows, params, coords_now, coords_before, ref, burning, basis, edges):
    cells, modes = basis.shape[1:]
    tiles = cells // TILE
    per = TILE // EDGE
    last = cells // EDGE - 1
    smem = pl.BlockSpec(memory_space=pltpu.SMEM)
    vmem = pl.BlockSpec(memory_space=pltpu.VMEM)
    half = modes // 2
    return pl.pallas_call(
        main_kernel,
        grid=(2, tiles),
        out_shape=[
            jax.ShapeDtypeStruct((2, cells, modes), jnp.bfloat16),
            jax.ShapeDtypeStruct((2, cells), jnp.float32),
            jax.ShapeDtypeStruct((packed_rows, LANES), jnp.float32),
        ],
        in_specs=[smem] * 3
        + [vmem] * 4
        + [
            pl.BlockSpec((2, TILE, modes), lambda p, i: (0, i, 0)),
            pl.BlockSpec((2, EDGE, modes), lambda p, i: (0, jnp.maximum(i * per - 1, 0), 0)),
            pl.BlockSpec((2, EDGE, modes), lambda p, i: (0, jnp.minimum((i + 1) * per, last), 0)),
        ]
        + [vmem] * 4,
        out_specs=[
            pl.BlockSpec((2, TILE, modes), lambda p, i: (0, i * p, 0)),
            vmem,
            vmem,
        ],
        scratch_shapes=[
            pltpu.VMEM((8, cells + 2 * LANES), jnp.float32),
            pltpu.VMEM((cells, 8), jnp.float32),
            pltpu.VMEM((16, cells), jnp.float32),
            pltpu.VMEM((2, TILE + 16, modes), jnp.float32),
            pltpu.VMEM((half, modes), jnp.float32),
            pltpu.VMEM((half, half), jnp.float32),
            pltpu.VMEM((1, modes), jnp.float32),
        ],
        compiler_params=pltpu.CompilerParams(vmem_limit_bytes=48 * 2**20),
    )(*params, coords_now, coords_before, ref, burning, basis, basis, basis, *edges)


def sum_kernel(n, part, out, arrived, gathered, send_a, recv_a, send_b, recv_b):
    me = lax.axis_index("space")
    size = part.shape[0] // n
    barrier = pltpu.get_barrier_semaphore()

    def greet(o, carry):
        pl.semaphore_signal(
            barrier, inc=1, device_id={"space": lax.rem(me + o, n)}, device_id_type=MESH
        )
        return carry

    lax.fori_loop(1, n, greet, 0)
    pl.semaphore_wait(barrier, n - 1)

    def span(d):
        return pl.ds(pl.multiple_of(d * size, 8), size)

    def scatter(o):
        to = lax.rem(me + o, n)
        return pltpu.make_async_remote_copy(
            src_ref=part.at[span(to)],
            dst_ref=arrived.at[o - 1],
            send_sem=send_a.at[o - 1],
            recv_sem=recv_a.at[o - 1],
            device_id={"space": to},
            device_id_type=MESH,
        )

    def gather(o, owner):
        return pltpu.make_async_remote_copy(
            src_ref=gathered.at[span(owner)],
            dst_ref=gathered.at[span(owner)],
            send_sem=send_b.at[o - 1],
            recv_sem=recv_b.at[o - 1],
            device_id={"space": lax.rem(me + o, n)},
            device_id_type=MESH,
        )

    def start_scatter(o, carry):
        scatter(o).start()
        return carry

    def take(o, total):
        scatter(o).wait_recv()
        return total + arrived[o - 1]

    def start_gather(o, carry):
        gather(o, me).start()
        return carry

    def finish(o, carry):
        scatter(o).wait_send()
        gather(o, me).wait_send()
        gather(o, lax.rem(me + n - o, n)).wait_recv()
        return carry

    lax.fori_loop(1, n, start_scatter, 0)
    gathered[span(me), :] = lax.fori_loop(1, n, take, part[span(me), :])
    lax.fori_loop(1, n, start_gather, 0)
    lax.fori_loop(1, n, finish, 0)
    out[...] = gathered[...]


def sum_over_space(n, part):
    rows = part.shape[0]
    dma = pltpu.SemaphoreType.DMA((n - 1,))
    vmem = pl.BlockSpec(memory_space=pltpu.VMEM)
    return pl.pallas_call(
        functools.partial(sum_kernel, n),
        out_shape=jax.ShapeDtypeStruct(part.shape, jnp.float32),
        in_specs=[vmem],
        out_specs=vmem,
        scratch_shapes=[
            pltpu.VMEM((n - 1, rows // n, LANES), jnp.float32),
            pltpu.VMEM(part.shape, jnp.float32),
            dma,
            dma,
            dma,
            dma,
        ],
        compiler_params=pltpu.CompilerParams(
            collective_id=1, has_side_effects=True, vmem_limit_bytes=32 * 2**20
        ),
    )(part)


PANEL = 8


def factor_panel(work, p, scaled, plain):
    first = p * PANEL
    rows = work[first : first + PANEL, :]
    a = [rows[i : i + 1, 0:LANES] for i in range(PANEL)]
    w = [rows[i : i + 1, LANES:] for i in range(PANEL)]
    s = {
        (i, j): jnp.broadcast_to(a[i][:, first + j : first + j + 1], (1, LANES))
        for i in range(PANEL)
        for j in range(i, PANEL)
    }
    for k in range(PANEL):
        inverse = 1.0 / s[k, k]
        for i in range(k + 1, PANEL):
            m = s[k, i] * inverse
            for j in range(i, PANEL):
                s[i, j] = s[i, j] - m * s[k, j]
            a[i] = a[i] - m * a[k]
            w[i] = w[i] - m * w[k]
        plain[first + k : first + k + 1, 0:LANES] = a[k]
        plain[first + k : first + k + 1, LANES:] = w[k]
        scaled[first + k : first + k + 1, 0:LANES] = a[k] * inverse
        scaled[first + k : first + k + 1, LANES:] = w[k] * inverse
    below = first + PANEL
    if below < LANES:
        change = tn_dot(
            scaled[first:below, 0:LANES], plain[first:below, :], HIGH
        )
        work[below:, :] = work[below:, :] - change[below:, :]


def solve_kernel(modes, packed, out, blocks, work, scaled, plain):
    count = modes // LANES
    place = {}
    for i in range(count):
        for j in range(i, count):
            place[i, j] = len(place)
            blocks[place[i, j]] = packed[place[i, j] * LANES : (place[i, j] + 1) * LANES, :]
    used = len(place) * LANES
    b = [packed[used + i : used + i + 1, :] for i in range(count)]
    row = lax.broadcasted_iota(jnp.int32, (LANES, LANES), 0)
    col = lax.broadcasted_iota(jnp.int32, (LANES, LANES), 1)
    eye = jnp.where(row == col, 1.0, 0.0).astype(jnp.float32)
    z, forward = [], {}
    for k in range(count):
        work[:, 0:LANES] = blocks[place[k, k]]
        work[:, LANES:] = eye
        for p in range(LANES // PANEL):
            factor_panel(work, p, scaled, plain)
        inverse = tn_dot(scaled[:, LANES:], plain[:, LANES:], HIGH)
        z.append(jnp.dot(b[k], inverse, precision=HIGH, preferred_element_type=jnp.float32))
        for j in range(k + 1, count):
            forward[k, j] = jnp.dot(
                inverse, blocks[place[k, j]], precision=HIGH, preferred_element_type=jnp.float32
            )
        for j in range(k + 1, count):
            b[j] = b[j] - jnp.dot(
                z[k], blocks[place[k, j]], precision=HIGH, preferred_element_type=jnp.float32
            )
            for i in range(k + 1, j + 1):
                blocks[place[i, j]] = blocks[place[i, j]] - tn_dot(
                    blocks[place[k, i]], forward[k, j], HIGH
                )
    x = [None] * count
    for k in reversed(range(count)):
        x[k] = z[k]
        for j in range(k + 1, count):
            x[k] = x[k] - nt_dot(x[j], forward[k, j], HIGH)
        out[:, k * LANES : (k + 1) * LANES] = -x[k]


def solve(modes, packed):
    count = modes // LANES
    vmem = pl.BlockSpec(memory_space=pltpu.VMEM)
    return pl.pallas_call(
        functools.partial(solve_kernel, modes),
        out_shape=jax.ShapeDtypeStruct((1, modes), jnp.float32),
        in_specs=[vmem],
        out_specs=vmem,
        scratch_shapes=[
            pltpu.VMEM((count * (count + 1) // 2, LANES, LANES), jnp.float32),
            pltpu.VMEM((LANES, 2 * LANES), jnp.float32),
            pltpu.VMEM((LANES, 2 * LANES), jnp.float32),
            pltpu.VMEM((LANES, 2 * LANES), jnp.float32),
        ],
        compiler_params=pltpu.CompilerParams(vmem_limit_bytes=32 * 2**20),
    )(packed)


def on_device(
    basis_rows,
    reference_state,
    burning,
    coords_now,
    coords_before,
    diffusivity,
    advection,
    reaction_rate,
):
    n = lax.axis_size("space")
    modes = basis_rows.shape[2]
    blocks = modes // LANES
    needed = blocks * (blocks + 1) // 2 * LANES + 8
    share = -(-needed // (8 * n)) * 8
    edges = halo(n, basis_rows, reference_state)
    jacobian, residual, packed = assemble(
        share * n,
        (diffusivity, advection, reaction_rate),
        coords_now,
        coords_before,
        reference_state,
        burning[None],
        basis_rows,
        edges,
    )
    update = solve(modes, sum_over_space(n, packed))
    return (jacobian[None], residual[None], update)


def solution(mesh):
    in_specs = (
        P(None, "space", None),
        P(None, "space"),
        P("space"),
        P("inst", None),
        P("inst", None),
        P("inst"),
        P("inst"),
        P("inst"),
    )
    out_specs = (P("inst", None, "space", None), P("inst", None, "space"), P("inst", None))
    return jax.shard_map(
        on_device, mesh=mesh, in_specs=in_specs, out_specs=out_specs, check_vma=False
    )
```

profile of v0, /device:TPU:0, one launch (start us, length us, event | category | flops | bytes accessed | tf_op | source)
XLA Modules:
  0.0 103.5 jit_solution(2102994910321554473)
XLA Ops:
  0.6 0.0 copy-start
  0.6 0.0 copy-start.5
  0.7 0.0 copy-start.4
  0.7 0.0 copy-start.3
  2.6 8.6 %shard_map.103 = (bf16[2,16,512]{2,1,0:T(8,128)(2,1)}, bf16[2,16,512]{2,1,0:T(8,128)(2,1)}, f32[2,128]{1,0:T(2,128)}, f32[2,128]{1,0:T(2,128)}) custom-call(bf16[2,3072,512]{2,1,0:T(8,128)(2,1)} %after_rows.1, f32[2,3072]{1,0:T(2,128)} %ref_ref.1), custom_call_target="tpu_custom_call" | custom-call | tf_op jit(solution)/shard_map/pallas_call | solution.py:98
  11.3 0.0 copy-done
  11.3 0.0 copy-done.5
  11.3 0.0 copy-done.4
  11.3 0.0 copy-done.3
  11.3 0.0 copy-start.1
  11.3 0.7 copy-done.1
  12.1 0.0 copy-start.2
  12.1 0.8 copy-done.2
  12.8 0.0 copy-start.6
  12.8 0.6 copy-done.6
  13.5 0.0 copy-start.7
  13.5 0.6 copy-done.7
  14.1 20.0 %shard_map.104 = (bf16[2,3072,512]{2,1,0:T(8,128)(2,1)}, f32[2,3072]{1,0:T(2,128)}, f32[1344,128]{1,0:T(8,128)S(1)}) custom-call(f32[1]{0:T(128)S(6)} %copy.11.diffusivity, f32[1]{0:T(128)S(6)} %copy.12.advection, f32[1]{0:T(128)S(6)} %copy.13.rate, f32[1,512]{1,0:T(1,128)S(1)} %copy-done.4, f32[1,512]{1,0:T(1,128)S(1)} %copy-done.5, f32[2,3072]{1,0:T(2,128)S(1)} %copy-done, ...), custom_call_target="tpu_custom_call" | custom-call | tf_op jit(solution)/shard_map/pallas_call | solution.py:251
  34.1 32.4 %shard_map.105.packed = f32[1344,128]{1,0:T(8,128)S(1)} custom-call(f32[1344,128]{1,0:T(8,128)S(1)} %get-tuple-element.16.part), custom_call_target="tpu_custom_call" | custom-call | tf_op jit(solution)/shard_map/pallas_call | solution.py:352
  66.5 37.0 %shard_map.106 = f32[1,512]{1,0:T(1,128)} custom-call(f32[1344,128]{1,0:T(8,128)S(1)} %shard_map.105.packed), custom_call_target="tpu_custom_call" | custom-call | tf_op jit(solution)/shard_map/pallas_call | solution.py:447
Async XLA Ops:
  0.6 10.6 %copy-start = (f32[2,3072]{1,0:T(2,128)S(1)}, f32[2,3072]{1,0:T(2,128)}, u32[]{:S(2)}) copy-start(f32[2,3072]{1,0:T(2,128)} %ref_ref.1) | copy-start | bytes 73732
  0.6 10.6 %copy-start.5 = (f32[1,512]{1,0:T(1,128)S(1)}, f32[1,512]{1,0:T(1,128)}, u32[]{:S(2)}) copy-start(f32[1,512]{1,0:T(1,128)} %before_ref.1) | copy-start | bytes 6148
  0.7 10.6 %copy-start.4 = (f32[1,512]{1,0:T(1,128)S(1)}, f32[1,512]{1,0:T(1,128)}, u32[]{:S(2)}) copy-start(f32[1,512]{1,0:T(1,128)} %now_ref.1) | copy-start | bytes 6148
  0.7 10.6 %copy-start.3 = (s32[3072]{0:T(1024)S(1)}, s32[3072]{0:T(1024)}, u32[]{:S(2)}) copy-start(s32[3072]{0:T(1024)} %param.10) | copy-start | bytes 36868
  11.3 0.8 copy-start.1
  12.1 0.8 copy-start.2
  12.8 0.6 copy-start.6
  13.5 0.6 copy-start.7
where the time goes:
time: 104 us
  Pallas kernels  98 us (94%)
  local copies, waits for them, and re-layouts  2.79 us (3%)
  between operations  2.69 us (3%)
    pallas_call x1, Pallas kernels, solve(): pl.pallas_call(functools.partial(solve_kernel, modes), out_shape=jax.Shap...  37 us
    pallas_call x1, Pallas kernels, sum_over_space(): pl.pallas_call(functools.partial(sum_kernel, n), out_shape=jax.ShapeDtype...  32.4 us
    pallas_call x1, Pallas kernels, assemble(): pl.pallas_call(main_kernel, grid=(2, tiles), out_shape=[jax.ShapeDtypeStr...  20 us
    pallas_call x1, Pallas kernels, halo(): pl.pallas_call(functools.partial(halo_kernel, n), out_shape=[jax.ShapeDty...  8.63 us
    unnamed x16, local copies, waits for them, and re-layouts  2.79 us

commit v1 on v0

--- a/solution.py
+++ b/solution.py
@@ -14,6 +14,8 @@
 LANES = 128
 EDGE = 16
 HIGH = lax.Precision.HIGHEST
+PANEL = 8
+RIGHT_STAGE = 1
 
 
 def tn_dot(a, b, precision=None):
@@ -111,7 +113,7 @@
 
 
 def main_kernel(
-    diffusivity, advection, rate, now_ref, before_ref, ref_ref, burn_ref, basis, before_rows,
+    stages, diffusivity, advection, rate, now_ref, before_ref, ref_ref, burn_ref, basis, before_rows,
     after_rows, low_b, high_b, low_r, high_r,
     jac, res_out, packed,
     state, coef, resid, wide, top, bottom, right,
@@ -223,24 +225,22 @@
 
     @pl.when((phase == 1) & (tile == tiles - 1))
     def _():
-        blocks = modes // LANES
-        spot = 0
-        for i in range(blocks):
-            for j in range(i, blocks):
+        packed[...] = jnp.zeros_like(packed)
+        for stage, (offset, _) in enumerate(stages):
+            j = stage
+            for i in range(j + 1):
                 if i * LANES < half:
                     block = top[i * LANES : (i + 1) * LANES, j * LANES : (j + 1) * LANES]
                 else:
-                    a, b = i * LANES - half, j * LANES - half
-                    block = bottom[a : a + LANES, b : b + LANES]
-                packed[spot * LANES : (spot + 1) * LANES, :] = block
-                spot += 1
-        used = spot * LANES
-        packed[used:, :] = jnp.zeros((packed.shape[0] - used, LANES), jnp.float32)
-        for i in range(blocks):
+                    first, second = i * LANES - half, j * LANES - half
+                    block = bottom[first : first + LANES, second : second + LANES]
+                packed[offset + i * LANES : offset + (i + 1) * LANES, :] = block
+        used = stages[RIGHT_STAGE][0] + (RIGHT_STAGE + 1) * LANES
+        for i in range(modes // LANES):
             packed[used + i : used + i + 1, :] = right[:, i * LANES : (i + 1) * LANES]
 
 
-def assemble(packed_rows, params, coords_now, coords_before, ref, burning, basis, edges):
+def assemble(stages, packed_rows, params, coords_now, coords_before, ref, burning, basis, edges):
     cells, modes = basis.shape[1:]
     tiles = cells // TILE
     per = TILE // EDGE
@@ -248,8 +248,12 @@
     smem = pl.BlockSpec(memory_space=pltpu.SMEM)
     vmem = pl.BlockSpec(memory_space=pltpu.VMEM)
     half = modes // 2
+
+    def whole(array):
+        return pl.BlockSpec(array.shape, lambda p, i: (0,) * array.ndim)
+
     return pl.pallas_call(
-        main_kernel,
+        functools.partial(main_kernel, stages),
         grid=(2, tiles),
         out_shape=[
             jax.ShapeDtypeStruct((2, cells, modes), jnp.bfloat16),
@@ -257,13 +261,13 @@
             jax.ShapeDtypeStruct((packed_rows, LANES), jnp.float32),
         ],
         in_specs=[smem] * 3
-        + [vmem] * 4
+        + [whole(coords_now), whole(coords_before), whole(ref), whole(burning)]
         + [
             pl.BlockSpec((2, TILE, modes), lambda p, i: (0, i, 0)),
             pl.BlockSpec((2, EDGE, modes), lambda p, i: (0, jnp.maximum(i * per - 1, 0), 0)),
             pl.BlockSpec((2, EDGE, modes), lambda p, i: (0, jnp.minimum((i + 1) * per, last), 0)),
         ]
-        + [vmem] * 4,
+        + [whole(edge) for edge in edges],
         out_specs=[
             pl.BlockSpec((2, TILE, modes), lambda p, i: (0, i * p, 0)),
             vmem,
@@ -282,9 +286,21 @@
     )(*params, coords_now, coords_before, ref, burning, basis, basis, basis, *edges)
 
 
-def sum_kernel(n, part, out, arrived, gathered, send_a, recv_a, send_b, recv_b):
+def layout(n, modes):
+    stages, offset = [], 0
+    for j in range(modes // LANES):
+        needed = (j + 1) * LANES + (8 if j == RIGHT_STAGE else 0)
+        size = -(-needed // (8 * n)) * 8
+        stages.append((offset, size))
+        offset += size * n
+    return tuple(stages), offset
+
+
+def sum_solve_kernel(
+    n, stages, modes, part, out,
+    arrived, total, work, panel_a, panel_w, plain, scaled, send_a, recv_a, send_b, recv_b,
+):
     me = lax.axis_index("space")
-    size = part.shape[0] // n
     barrier = pltpu.get_barrier_semaphore()
 
     def greet(o, carry):
@@ -296,67 +312,170 @@
     lax.fori_loop(1, n, greet, 0)
     pl.semaphore_wait(barrier, n - 1)
 
-    def span(d):
-        return pl.ds(pl.multiple_of(d * size, 8), size)
-
-    def scatter(o):
+    def span(stage, d):
+        offset, size = stages[stage]
+        return pl.ds(pl.multiple_of(offset + d * size, 8), size)
+
+    def scatter(stage, o):
         to = lax.rem(me + o, n)
+        offset, size = stages[stage]
         return pltpu.make_async_remote_copy(
-            src_ref=part.at[span(to)],
-            dst_ref=arrived.at[o - 1],
-            send_sem=send_a.at[o - 1],
-            recv_sem=recv_a.at[o - 1],
+            src_ref=part.at[span(stage, to)],
+            dst_ref=arrived.at[o - 1, pl.ds(offset // n, size)],
+            send_sem=send_a.at[stage, o - 1],
+            recv_sem=recv_a.at[stage, o - 1],
             device_id={"space": to},
             device_id_type=MESH,
         )
 
-    def gather(o, owner):
+    def gather(stage, o, owner):
         return pltpu.make_async_remote_copy(
-            src_ref=gathered.at[span(owner)],
-            dst_ref=gathered.at[span(owner)],
-            send_sem=send_b.at[o - 1],
-            recv_sem=recv_b.at[o - 1],
+            src_ref=total.at[span(stage, owner)],
+            dst_ref=total.at[span(stage, owner)],
+            send_sem=send_b.at[stage, o - 1],
+            recv_sem=recv_b.at[stage, o - 1],
             device_id={"space": lax.rem(me + o, n)},
             device_id_type=MESH,
         )
 
-    def start_scatter(o, carry):
-        scatter(o).start()
+    def start_sum(stage):
+        def body(o, carry):
+            scatter(stage, o).start()
+            return carry
+
+        lax.fori_loop(1, n, body, 0)
+
+    def pass_on(stage):
+        offset, size = stages[stage]
+
+        def add(o, sums):
+            scatter(stage, o).wait_recv()
+            return sums + arrived[o - 1, offset // n : offset // n + size, :]
+
+        def send(o, carry):
+            gather(stage, o, me).start()
+            return carry
+
+        total[span(stage, me), :] = lax.fori_loop(1, n, add, part[span(stage, me), :])
+        lax.fori_loop(1, n, send, 0)
+
+    def end_sum(stage):
+        def body(o, carry):
+            scatter(stage, o).wait_send()
+            gather(stage, o, me).wait_send()
+            gather(stage, o, lax.rem(me + n - o, n)).wait_recv()
+            return carry
+
+        lax.fori_loop(1, n, body, 0)
+
+    lane = lax.broadcasted_iota(jnp.int32, (PANEL, LANES), 1)
+
+    def factor_panel(p, carry):
+        first = pl.multiple_of(p * PANEL, PANEL)
+        rows_a = work[pl.ds(first, PANEL), 0:LANES]
+        rows_w = work[pl.ds(first, PANEL), LANES:]
+        turned = pltpu.roll(rows_a, LANES - first, 1)
+        a = [rows_a[i : i + 1, :] for i in range(PANEL)]
+        w = [rows_w[i : i + 1, :] for i in range(PANEL)]
+        s = {
+            (i, j): jnp.broadcast_to(turned[i : i + 1, j : j + 1], (1, LANES))
+            for i in range(PANEL)
+            for j in range(i, PANEL)
+        }
+        for k in range(PANEL):
+            inverse = 1.0 / s[k, k]
+            for i in range(k + 1, PANEL):
+                m = s[k, i] * inverse
+                for j in range(i, PANEL):
+                    s[i, j] = s[i, j] - m * s[k, j]
+                a[i] = a[i] - m * a[k]
+                w[i] = w[i] - m * w[k]
+            panel_a[k : k + 1, :] = a[k] * inverse
+            panel_w[k : k + 1, 0:LANES] = a[k]
+            panel_w[k : k + 1, LANES:] = w[k]
+            panel_w[PANEL + k : PANEL + k + 1, LANES:] = w[k] * inverse
+        both = panel_w[0:PANEL, :]
+        plain[pl.ds(first, PANEL), :] = both[:, LANES:]
+        scaled[pl.ds(first, PANEL), :] = panel_w[PANEL:, LANES:]
+        below = jnp.where(lane >= first + PANEL, panel_a[...], 0.0)
+        work[...] = work[...] - tn_dot(below, both, HIGH)
         return carry
 
-    def take(o, total):
-        scatter(o).wait_recv()
-        return total + arrived[o - 1]
-
-    def start_gather(o, carry):
-        gather(o, me).start()
-        return carry
-
-    def finish(o, carry):
-        scatter(o).wait_send()
-        gather(o, me).wait_send()
-        gather(o, lax.rem(me + n - o, n)).wait_recv()
-        return carry
-
-    lax.fori_loop(1, n, start_scatter, 0)
-    gathered[span(me), :] = lax.fori_loop(1, n, take, part[span(me), :])
-    lax.fori_loop(1, n, start_gather, 0)
-    lax.fori_loop(1, n, finish, 0)
-    out[...] = gathered[...]
-
-
-def sum_over_space(n, part):
+    def factor(low, high):
+        lax.fori_loop(low, high, factor_panel, 0)
+
+    def block(i, j):
+        return total[stages[j][0] + i * LANES : stages[j][0] + (i + 1) * LANES, :]
+
+    def dot(a, b):
+        return jnp.dot(a, b, precision=HIGH, preferred_element_type=jnp.float32)
+
+    count = modes // LANES
+    panels = LANES // PANEL
+    row = lax.broadcasted_iota(jnp.int32, (LANES, LANES), 0)
+    col = lax.broadcasted_iota(jnp.int32, (LANES, LANES), 1)
+    eye = jnp.where(row == col, 1.0, 0.0).astype(jnp.float32)
+
+    between = {(0, 4): [1], (0, 10): [2], (1, 6): [3]}
+    start_sum(0)
+    start_sum(1)
+    pass_on(0)
+    start_sum(2)
+    start_sum(3)
+
+    inverses, upper, forward, z, b = [], {}, {}, [], None
+    for k in range(count):
+        end_sum(k)
+        if k == RIGHT_STAGE:
+            used = stages[k][0] + (k + 1) * LANES
+            b = [total[used + i : used + i + 1, :] for i in range(count)]
+        for i in range(k + 1):
+            current = block(i, k)
+            for r in range(i):
+                current = current - tn_dot(upper[r, i], forward[r, k], HIGH)
+            if i < k:
+                upper[i, k] = current
+                forward[i, k] = dot(inverses[i], current)
+        work[:, 0:LANES] = current
+        work[:, LANES:] = eye
+        done = 0
+        for at in range(1, panels):
+            for stage in between.get((k, at), ()):
+                factor(done, at)
+                pass_on(stage)
+                done = at
+        factor(done, panels)
+        inverses.append(tn_dot(scaled[...], plain[...], HIGH))
+    for k in range(count):
+        current = b[k]
+        for r in range(k):
+            current = current - dot(z[r], upper[r, k])
+        z.append(dot(current, inverses[k]))
+    x = [None] * count
+    for k in reversed(range(count)):
+        x[k] = z[k]
+        for j in range(k + 1, count):
+            x[k] = x[k] - nt_dot(x[j], forward[k, j], HIGH)
+        out[:, k * LANES : (k + 1) * LANES] = -x[k]
+
+
+def sum_and_solve(n, stages, modes, part):
     rows = part.shape[0]
-    dma = pltpu.SemaphoreType.DMA((n - 1,))
+    dma = pltpu.SemaphoreType.DMA((len(stages), n - 1))
     vmem = pl.BlockSpec(memory_space=pltpu.VMEM)
     return pl.pallas_call(
-        functools.partial(sum_kernel, n),
-        out_shape=jax.ShapeDtypeStruct(part.shape, jnp.float32),
+        functools.partial(sum_solve_kernel, n, stages, modes),
+        out_shape=jax.ShapeDtypeStruct((1, modes), jnp.float32),
         in_specs=[vmem],
         out_specs=vmem,
         scratch_shapes=[
             pltpu.VMEM((n - 1, rows // n, LANES), jnp.float32),
-            pltpu.VMEM(part.shape, jnp.float32),
+            pltpu.VMEM((rows, LANES), jnp.float32),
+            pltpu.VMEM((LANES, 2 * LANES), jnp.float32),
+            pltpu.VMEM((PANEL, LANES), jnp.float32),
+            pltpu.VMEM((2 * PANEL, 2 * LANES), jnp.float32),
+            pltpu.VMEM((LANES, LANES), jnp.float32),
+            pltpu.VMEM((LANES, LANES), jnp.float32),
             dma,
             dma,
             dma,
@@ -366,97 +485,6 @@
             collective_id=1, has_side_effects=True, vmem_limit_bytes=32 * 2**20
         ),
     )(part)
-
-
-PANEL = 8
-
-
-def factor_panel(work, p, scaled, plain):
-    first = p * PANEL
-    rows = work[first : first + PANEL, :]
-    a = [rows[i : i + 1, 0:LANES] for i in range(PANEL)]
-    w = [rows[i : i + 1, LANES:] for i in range(PANEL)]
-    s = {
-        (i, j): jnp.broadcast_to(a[i][:, first + j : first + j + 1], (1, LANES))
-        for i in range(PANEL)
-        for j in range(i, PANEL)
-    }
-    for k in range(PANEL):
-        inverse = 1.0 / s[k, k]
-        for i in range(k + 1, PANEL):
-            m = s[k, i] * inverse
-            for j in range(i, PANEL):
-                s[i, j] = s[i, j] - m * s[k, j]
-            a[i] = a[i] - m * a[k]
-            w[i] = w[i] - m * w[k]
-        plain[first + k : first + k + 1, 0:LANES] = a[k]
-        plain[first + k : first + k + 1, LANES:] = w[k]
-        scaled[first + k : first + k + 1, 0:LANES] = a[k] * inverse
-        scaled[first + k : first + k + 1, LANES:] = w[k] * inverse
-    below = first + PANEL
-    if below < LANES:
-        change = tn_dot(
-            scaled[first:below, 0:LANES], plain[first:below, :], HIGH
-        )
-        work[below:, :] = work[below:, :] - change[below:, :]
-
-
-def solve_kernel(modes, packed, out, blocks, work, scaled, plain):
-    count = modes // LANES
-    place = {}
-    for i in range(count):
-        for j in range(i, count):
-            place[i, j] = len(place)
-            blocks[place[i, j]] = packed[place[i, j] * LANES : (place[i, j] + 1) * LANES, :]
-    used = len(place) * LANES
-    b = [packed[used + i : used + i + 1, :] for i in range(count)]
-    row = lax.broadcasted_iota(jnp.int32, (LANES, LANES), 0)
-    col = lax.broadcasted_iota(jnp.int32, (LANES, LANES), 1)
-    eye = jnp.where(row == col, 1.0, 0.0).astype(jnp.float32)
-    z, forward = [], {}
-    for k in range(count):
-        work[:, 0:LANES] = blocks[place[k, k]]
-        work[:, LANES:] = eye
-        for p in range(LANES // PANEL):
-            factor_panel(work, p, scaled, plain)
-        inverse = tn_dot(scaled[:, LANES:], plain[:, LANES:], HIGH)
-        z.append(jnp.dot(b[k], inverse, precision=HIGH, preferred_element_type=jnp.float32))
-        for j in range(k + 1, count):
-            forward[k, j] = jnp.dot(
-                inverse, blocks[place[k, j]], precision=HIGH, preferred_element_type=jnp.float32
-            )
-        for j in range(k + 1, count):
-            b[j] = b[j] - jnp.dot(
-                z[k], blocks[place[k, j]], precision=HIGH, preferred_element_type=jnp.float32
-            )
-            for i in range(k + 1, j + 1):
-                blocks[place[i, j]] = blocks[place[i, j]] - tn_dot(
-                    blocks[place[k, i]], forward[k, j], HIGH
-                )
-    x = [None] * count
-    for k in reversed(range(count)):
-        x[k] = z[k]
-        for j in range(k + 1, count):
-            x[k] = x[k] - nt_dot(x[j], forward[k, j], HIGH)
-        out[:, k * LANES : (k + 1) * LANES] = -x[k]
-
-
-def solve(modes, packed):
-    count = modes // LANES
-    vmem = pl.BlockSpec(memory_space=pltpu.VMEM)
-    return pl.pallas_call(
-        functools.partial(solve_kernel, modes),
-        out_shape=jax.ShapeDtypeStruct((1, modes), jnp.float32),
-        in_specs=[vmem],
-        out_specs=vmem,
-        scratch_shapes=[
-            pltpu.VMEM((count * (count + 1) // 2, LANES, LANES), jnp.float32),
-            pltpu.VMEM((LANES, 2 * LANES), jnp.float32),
-            pltpu.VMEM((LANES, 2 * LANES), jnp.float32),
-            pltpu.VMEM((LANES, 2 * LANES), jnp.float32),
-        ],
-        compiler_params=pltpu.CompilerParams(vmem_limit_bytes=32 * 2**20),
-    )(packed)
 
 
 def on_device(
@@ -471,12 +499,11 @@
 ):
     n = lax.axis_size("space")
     modes = basis_rows.shape[2]
-    blocks = modes // LANES
-    needed = blocks * (blocks + 1) // 2 * LANES + 8
-    share = -(-needed // (8 * n)) * 8
+    stages, packed_rows = layout(n, modes)
     edges = halo(n, basis_rows, reference_state)
     jacobian, residual, packed = assemble(
-        share * n,
+        stages,
+        packed_rows,
         (diffusivity, advection, reaction_rate),
         coords_now,
         coords_before,
@@ -485,7 +512,7 @@
         basis_rows,
         edges,
     )
-    update = solve(modes, sum_over_space(n, packed))
+    update = sum_and_solve(n, stages, modes, packed)
     return (jacobian[None], residual[None], update)
 
 

time: 104 us -> 93.4 us (0.90)
  Pallas kernels: 98 us -> 86.9 us
    pallas_call x3 -> x2, Pallas kernels: 89.4 us -> 78.3 us  [the longest x1 58.3 us: sum_and_solve(): pl.pallas_call(functools.partial(sum_solve_kernel, n, stages, modes), out...]
    unnamed x16 -> x17, local copies, waits for them, and re-layouts: 2.79 us -> 3.37 us
where the time goes in v1:
time: 93.4 us; the launch traced here: 93 us
  Pallas kernels  86.9 us (93%)
  local copies, waits for them, and re-layouts  3.37 us (4%)
  between operations  2.69 us (3%)
    pallas_call x1, Pallas kernels, sum_and_solve(): pl.pallas_call(functools.partial(sum_solve_kernel, n, stages, modes), out...  58.3 us
    pallas_call x1, Pallas kernels, assemble(): pl.pallas_call(functools.partial(main_kernel, stages), grid=(2, tiles), o...  20 us
    pallas_call x1, Pallas kernels, halo(): pl.pallas_call(functools.partial(halo_kernel, n), out_shape=[jax.ShapeDty...  8.63 us
    unnamed x17, local copies, waits for them, and re-layouts  3.37 us

profile of v1, /device:TPU:0, one launch (start us, length us, event | category | flops | bytes accessed | tf_op | source)
XLA Modules:
  0.0 93.0 jit_solution(13022768365396546905)
XLA Ops:
  0.6 0.0 copy-start
  0.6 0.0 copy-start.5
  0.7 0.0 copy-start.4
  0.7 0.0 copy-start.3
  2.6 8.6 %shard_map.103 = (bf16[2,16,512]{2,1,0:T(8,128)(2,1)}, bf16[2,16,512]{2,1,0:T(8,128)(2,1)}, f32[2,128]{1,0:T(2,128)}, f32[2,128]{1,0:T(2,128)}) custom-call(bf16[2,3072,512]{2,1,0:T(8,128)(2,1)} %after_rows.1, f32[2,3072]{1,0:T(2,128)} %ref_ref.1), custom_call_target="tpu_custom_call" | custom-call | tf_op jit(solution)/shard_map/pallas_call | solution.py:100
  11.3 0.0 copy-done
  11.3 0.0 copy-done.5
  11.3 0.0 copy-done.4
  11.3 0.0 copy-done.3
  11.3 0.0 copy-start.1
  11.3 0.7 copy-done.1
  12.1 0.0 copy-start.2
  12.1 0.8 copy-done.2
  12.8 0.0 copy-start.6
  12.8 0.6 copy-done.6
  13.5 0.0 copy-start.7
  13.5 0.6 copy-done.7
  14.1 20.0 %shard_map.104 = (bf16[2,3072,512]{2,1,0:T(8,128)(2,1)}, f32[2,3072]{1,0:T(2,128)}, f32[1344,128]{1,0:T(8,128)S(1)}) custom-call(f32[1]{0:T(128)S(6)} %copy.12.diffusivity, f32[1]{0:T(128)S(6)} %copy.13.advection, f32[1]{0:T(128)S(6)} %copy.14.rate, f32[1,512]{1,0:T(1,128)S(1)} %copy-done.4, f32[1,512]{1,0:T(1,128)S(1)} %copy-done.5, f32[2,3072]{1,0:T(2,128)S(1)} %copy-done, ...), custom_call_target="tpu_custom_call" | custom-call | tf_op jit(solution)/shard_map/pallas_call | solution.py:255
  34.1 58.3 %shard_map.105 = f32[1,512]{1,0:T(1,128)S(1)} custom-call(f32[1344,128]{1,0:T(8,128)S(1)} %get-tuple-element.16.part), custom_call_target="tpu_custom_call" | custom-call | tf_op jit(solution)/shard_map/pallas_call | solution.py:466
  92.4 0.6 copy.15
Async XLA Ops:
  0.6 10.6 %copy-start = (f32[2,3072]{1,0:T(2,128)S(1)}, f32[2,3072]{1,0:T(2,128)}, u32[]{:S(2)}) copy-start(f32[2,3072]{1,0:T(2,128)} %ref_ref.1) | copy-start | bytes 73732
  0.6 10.6 %copy-start.5 = (f32[1,512]{1,0:T(1,128)S(1)}, f32[1,512]{1,0:T(1,128)}, u32[]{:S(2)}) copy-start(f32[1,512]{1,0:T(1,128)} %before_ref.1) | copy-start | bytes 6148
  0.7 10.6 %copy-start.4 = (f32[1,512]{1,0:T(1,128)S(1)}, f32[1,512]{1,0:T(1,128)}, u32[]{:S(2)}) copy-start(f32[1,512]{1,0:T(1,128)} %now_ref.1) | copy-start | bytes 6148
  0.7 10.6 %copy-start.3 = (s32[3072]{0:T(1024)S(1)}, s32[3072]{0:T(1024)}, u32[]{:S(2)}) copy-start(s32[3072]{0:T(1024)} %param.10) | copy-start | bytes 36868
  11.3 0.8 copy-start.1
  12.1 0.8 copy-start.2
  12.8 0.6 copy-start.6
  13.5 0.6 copy-start.7

commit v2 on v1

--- a/solution.py
+++ b/solution.py
@@ -14,7 +14,7 @@
 LANES = 128
 EDGE = 16
 HIGH = lax.Precision.HIGHEST
-PANEL = 8
+PANEL = 16
 RIGHT_STAGE = 1
 
 
@@ -30,15 +30,19 @@
     )
 
 
-def halo_kernel(n, basis, ref, low_b, high_b, low_r, high_r, send, recv):
+def reciprocal(x):
+    guess = pl.reciprocal(x, approx=True)
+    guess = guess + guess * (1.0 - x * guess)
+    return guess + guess * (1.0 - x * guess)
+
+
+def halo_kernel(n, basis, ref, edge_b, edge_r, send, recv):
     me = lax.axis_index("space")
     cells = basis.shape[1]
     has_low, has_high = me > 0, me < n - 1
 
-    low_b[...] = jnp.zeros_like(low_b)
-    high_b[...] = jnp.zeros_like(high_b)
-    low_r[...] = jnp.zeros_like(low_r)
-    high_r[...] = jnp.zeros_like(high_r)
+    edge_b[...] = jnp.zeros_like(edge_b)
+    edge_r[...] = jnp.zeros_like(edge_r)
 
     barrier = pltpu.get_barrier_semaphore()
     for step in (1, n - 1):
@@ -61,12 +65,12 @@
         )
 
     to_up = [
-        copy(basis.at[:, pl.ds(cells - EDGE, EDGE), :], low_b, 0, up),
-        copy(ref.at[:, pl.ds(cells - LANES, LANES)], low_r, 1, up),
+        copy(basis.at[:, pl.ds(cells - EDGE, EDGE), :], edge_b.at[0], 0, up),
+        copy(ref.at[:, pl.ds(cells - LANES, LANES)], edge_r.at[0], 1, up),
     ]
     to_down = [
-        copy(basis.at[:, pl.ds(0, EDGE), :], high_b, 2, down),
-        copy(ref.at[:, pl.ds(0, LANES)], high_r, 3, down),
+        copy(basis.at[:, pl.ds(0, EDGE), :], edge_b.at[1], 2, down),
+        copy(ref.at[:, pl.ds(0, LANES)], edge_r.at[1], 3, down),
     ]
 
     @pl.when(has_high)
@@ -100,13 +104,11 @@
     return pl.pallas_call(
         functools.partial(halo_kernel, n),
         out_shape=[
-            jax.ShapeDtypeStruct((2, EDGE, modes), jnp.bfloat16),
-            jax.ShapeDtypeStruct((2, EDGE, modes), jnp.bfloat16),
-            jax.ShapeDtypeStruct((2, LANES), jnp.float32),
-            jax.ShapeDtypeStruct((2, LANES), jnp.float32),
+            jax.ShapeDtypeStruct((2, 2, EDGE, modes), jnp.bfloat16),
+            jax.ShapeDtypeStruct((2, 2, LANES), jnp.float32),
         ],
         in_specs=[pl.BlockSpec(memory_space=pl.ANY)] * 2,
-        out_specs=[vmem] * 4,
+        out_specs=[vmem] * 2,
         scratch_shapes=[pltpu.SemaphoreType.DMA((4,)), pltpu.SemaphoreType.DMA((4,))],
         compiler_params=pltpu.CompilerParams(collective_id=0, has_side_effects=True),
     )(basis, ref)
@@ -114,7 +116,7 @@
 
 def main_kernel(
     stages, diffusivity, advection, rate, now_ref, before_ref, ref_ref, burn_ref, basis, before_rows,
-    after_rows, low_b, high_b, low_r, high_r,
+    after_rows, edge_b, edge_r,
     jac, res_out, packed,
     state, coef, resid, wide, top, bottom, right,
 ):
@@ -144,13 +146,13 @@
             resid[...] = jnp.zeros_like(resid)
             lane = lax.broadcasted_iota(jnp.int32, (1, LANES), 1)
             for v in range(2):
-                low = nt_dot(vec, low_b[v])[0:1, EDGE - 1 : EDGE]
+                low = nt_dot(vec, edge_b[0, v])[0:1, EDGE - 1 : EDGE]
                 state[v : v + 1, 0:LANES] = jnp.where(
-                    lane == LANES - 1, low_r[v : v + 1, :] + low, 0.0
+                    lane == LANES - 1, edge_r[0, v : v + 1, :] + low, 0.0
                 )
-                high = nt_dot(vec, high_b[v])[0:1, 0:1]
+                high = nt_dot(vec, edge_b[1, v])[0:1, 0:1]
                 state[v : v + 1, LANES + cells : 2 * LANES + cells] = jnp.where(
-                    lane == 0, high_r[v : v + 1, :] + high, 0.0
+                    lane == 0, edge_r[1, v : v + 1, :] + high, 0.0
                 )
 
         for v in range(2):
@@ -191,9 +193,9 @@
     def _():
         for v in range(2):
             wide[v, 8 : 8 + TILE, :] = basis[v].astype(jnp.float32)
-            before = jnp.where(tile == 0, low_b[v], before_rows[v]).astype(jnp.float32)
+            before = jnp.where(tile == 0, edge_b[0, v], before_rows[v]).astype(jnp.float32)
             wide[v, 0:8, :] = before[EDGE - 8 : EDGE]
-            after = jnp.where(tile == tiles - 1, high_b[v], after_rows[v]).astype(jnp.float32)
+            after = jnp.where(tile == tiles - 1, edge_b[1, v], after_rows[v]).astype(jnp.float32)
             wide[v, 8 + TILE : 16 + TILE, :] = after[0:8]
         base = 1.0 + 2.0 * h * nu + h * c
         to_left = -h * (nu + c)
@@ -383,7 +385,7 @@
             for j in range(i, PANEL)
         }
         for k in range(PANEL):
-            inverse = 1.0 / s[k, k]
+            inverse = reciprocal(s[k, k])
             for i in range(k + 1, PANEL):
                 m = s[k, i] * inverse
                 for j in range(i, PANEL):
@@ -416,16 +418,16 @@
     col = lax.broadcasted_iota(jnp.int32, (LANES, LANES), 1)
     eye = jnp.where(row == col, 1.0, 0.0).astype(jnp.float32)
 
-    between = {(0, 4): [1], (0, 10): [2], (1, 6): [3]}
+    between = {(0, panels // 4): [1], (0, panels * 3 // 4): [2], (1, panels // 2): [3]}
     start_sum(0)
+    pass_on(0)
     start_sum(1)
-    pass_on(0)
-    start_sum(2)
-    start_sum(3)
 
     inverses, upper, forward, z, b = [], {}, {}, [], None
     for k in range(count):
         end_sum(k)
+        if k + 2 < count:
+            start_sum(k + 2)
         if k == RIGHT_STAGE:
             used = stages[k][0] + (k + 1) * LANES
             b = [total[used + i : used + i + 1, :] for i in range(count)]

time: 93.4 us -> 88.3 us (0.945)
  Pallas kernels: 86.9 us -> 83.2 us
  local copies, waits for them, and re-layouts: 3.37 us -> 2.09 us
    pallas_call x1, Pallas kernels: 58.3 us -> 54.6 us  [sum_and_solve(): pl.pallas_call(functools.partial(sum_solve_kernel, n, stages, modes), out...]
    unnamed x17 -> x13, local copies, waits for them, and re-layouts: 3.37 us -> 2.09 us
where the time goes in v2:
time: 88.3 us; the launch traced here: 87.9 us
  Pallas kernels  83.2 us (94%)
  between operations  2.69 us (3%)
  local copies, waits for them, and re-layouts  2.09 us (2%)
    pallas_call x1, Pallas kernels, sum_and_solve(): pl.pallas_call(functools.partial(sum_solve_kernel, n, stages, modes), out...  54.6 us
    pallas_call x1, Pallas kernels, assemble(): pl.pallas_call(functools.partial(main_kernel, stages), grid=(2, tiles), o...  20 us
    pallas_call x1, Pallas kernels, halo(): pl.pallas_call(functools.partial(halo_kernel, n), out_shape=[jax.ShapeDty...  8.62 us
    unnamed x13, local copies, waits for them, and re-layouts  2.09 us

profile of v2, /device:TPU:0, one launch (start us, length us, event | category | flops | bytes accessed | tf_op | source)
XLA Modules:
  0.0 87.9 jit_solution(10730467221205963229)
XLA Ops:
  0.6 0.0 copy-start
  0.6 0.0 copy-start.4
  0.7 0.0 copy-start.3
  0.7 0.0 copy-start.2
  2.6 8.6 %shard_map.103 = (bf16[2,2,16,512]{3,2,1,0:T(8,128)(2,1)}, f32[2,2,128]{2,1,0:T(2,128)}) custom-call(bf16[2,3072,512]{2,1,0:T(8,128)(2,1)} %after_rows.1, f32[2,3072]{1,0:T(2,128)} %ref_ref.1), custom_call_target="tpu_custom_call" | custom-call | tf_op jit(solution)/shard_map/pallas_call | solution.py:104
  11.3 0.0 copy-done
  11.3 0.0 copy-done.4
  11.3 0.0 copy-done.3
  11.3 0.0 copy-done.2
  11.3 0.0 copy-start.1
  11.3 0.8 copy-done.1
  12.2 0.0 copy-start.5
  12.2 0.7 copy-done.5
  12.8 20.0 %shard_map.104 = (bf16[2,3072,512]{2,1,0:T(8,128)(2,1)}, f32[2,3072]{1,0:T(2,128)}, f32[1344,128]{1,0:T(8,128)S(1)}) custom-call(f32[1]{0:T(128)S(6)} %copy.12.diffusivity, f32[1]{0:T(128)S(6)} %copy.13.advection, f32[1]{0:T(128)S(6)} %copy.14.rate, f32[1,512]{1,0:T(1,128)S(1)} %copy-done.3, f32[1,512]{1,0:T(1,128)S(1)} %copy-done.4, f32[2,3072]{1,0:T(2,128)S(1)} %copy-done, ...), custom_call_target="tpu_custom_call" | custom-call | tf_op jit(solution)/shard_map/pallas_call | solution.py:257
  32.8 54.6 %shard_map.105 = f32[1,512]{1,0:T(1,128)S(1)} custom-call(f32[1344,128]{1,0:T(8,128)S(1)} %get-tuple-element.12.part), custom_call_target="tpu_custom_call" | custom-call | tf_op jit(solution)/shard_map/pallas_call | solution.py:468
  87.4 0.6 copy.15
Async XLA Ops:
  0.6 10.6 %copy-start = (f32[2,3072]{1,0:T(2,128)S(1)}, f32[2,3072]{1,0:T(2,128)}, u32[]{:S(2)}) copy-start(f32[2,3072]{1,0:T(2,128)} %ref_ref.1) | copy-start | bytes 73732
  0.6 10.6 %copy-start.4 = (f32[1,512]{1,0:T(1,128)S(1)}, f32[1,512]{1,0:T(1,128)}, u32[]{:S(2)}) copy-start(f32[1,512]{1,0:T(1,128)} %before_ref.1) | copy-start | bytes 6148
  0.7 10.6 %copy-start.3 = (f32[1,512]{1,0:T(1,128)S(1)}, f32[1,512]{1,0:T(1,128)}, u32[]{:S(2)}) copy-start(f32[1,512]{1,0:T(1,128)} %now_ref.1) | copy-start | bytes 6148
  0.7 10.6 %copy-start.2 = (s32[3072]{0:T(1024)S(1)}, s32[3072]{0:T(1024)}, u32[]{:S(2)}) copy-start(s32[3072]{0:T(1024)} %param.10) | copy-start | bytes 36868
  11.3 0.8 copy-start.1
  12.2 0.7 copy-start.5

commit v3 on v2

--- a/solution.py
+++ b/solution.py
@@ -36,20 +36,26 @@
     return guess + guess * (1.0 - x * guess)
 
 
-def halo_kernel(n, basis, ref, edge_b, edge_r, send, recv):
+def halo_kernel(
+    n, now_ref, before_ref, ref_ref, rows, basis, ref, edge_b, state, land_b, land_r, send, recv
+):
+    tile, tiles = pl.program_id(0), pl.num_programs(0)
     me = lax.axis_index("space")
-    cells = basis.shape[1]
+    cells, modes = basis.shape[1:]
     has_low, has_high = me > 0, me < n - 1
-
-    edge_b[...] = jnp.zeros_like(edge_b)
-    edge_r[...] = jnp.zeros_like(edge_r)
-
-    barrier = pltpu.get_barrier_semaphore()
-    for step in (1, n - 1):
-        pl.semaphore_signal(
-            barrier, inc=1, device_id={"space": lax.rem(me + step, n)}, device_id_type=MESH
-        )
-    pl.semaphore_wait(barrier, 2)
+    first, last = tile == 0, tile == tiles - 1
+
+    @pl.when(first)
+    def _():
+        land_b[...] = jnp.zeros_like(land_b)
+        land_r[...] = jnp.zeros_like(land_r)
+        state[...] = jnp.zeros_like(state)
+        barrier = pltpu.get_barrier_semaphore()
+        for step in (1, n - 1):
+            pl.semaphore_signal(
+                barrier, inc=1, device_id={"space": lax.rem(me + step, n)}, device_id_type=MESH
+            )
+        pl.semaphore_wait(barrier, 2)
 
     up = {"space": lax.rem(me + 1, n)}
     down = {"space": lax.rem(me + n - 1, n)}
@@ -65,103 +71,116 @@
         )
 
     to_up = [
-        copy(basis.at[:, pl.ds(cells - EDGE, EDGE), :], edge_b.at[0], 0, up),
-        copy(ref.at[:, pl.ds(cells - LANES, LANES)], edge_r.at[0], 1, up),
+        copy(basis.at[:, pl.ds(cells - EDGE, EDGE), :], land_b.at[0], 0, up),
+        copy(ref.at[:, pl.ds(cells - LANES, LANES)], land_r.at[0], 1, up),
     ]
     to_down = [
-        copy(basis.at[:, pl.ds(0, EDGE), :], edge_b.at[1], 2, down),
-        copy(ref.at[:, pl.ds(0, LANES)], edge_r.at[1], 3, down),
+        copy(basis.at[:, pl.ds(0, EDGE), :], land_b.at[1], 2, down),
+        copy(ref.at[:, pl.ds(0, LANES)], land_r.at[1], 3, down),
     ]
 
-    @pl.when(has_high)
+    @pl.when(first & has_high)
     def _():
         for c in to_up:
             c.start()
 
-    @pl.when(has_low)
+    @pl.when(first & has_low)
     def _():
         for c in to_down:
             c.start()
 
-    @pl.when(has_high)
+    row = lax.broadcasted_iota(jnp.int32, (16, modes), 0)
+    now = now_ref[...]
+    vec = jnp.where(row == 0, now, jnp.where(row == 1, now - before_ref[...], 0.0))
+    vec = vec.astype(jnp.bfloat16)
+    here = pl.ds(pl.multiple_of(tile * TILE, TILE), TILE)
+    inner = pl.ds(pl.multiple_of(tile * TILE + LANES, LANES), TILE)
+    for v in range(2):
+        both = nt_dot(vec, rows[v])
+        state[v : v + 1, inner] = both[0:1] + ref_ref[v : v + 1, here]
+        state[v + 2 : v + 3, inner] = both[1:2]
+
+    @pl.when(last & has_high)
     def _():
         for c in to_up:
             c.wait_send()
         for c in to_down:
             c.wait_recv()
 
-    @pl.when(has_low)
+    @pl.when(last & has_low)
     def _():
         for c in to_down:
             c.wait_send()
         for c in to_up:
             c.wait_recv()
 
-
-def halo(n, basis, ref):
-    modes = basis.shape[2]
-    vmem = pl.BlockSpec(memory_space=pltpu.VMEM)
+    @pl.when(last)
+    def _():
+        edge_b[...] = land_b[...]
+        lane = lax.broadcasted_iota(jnp.int32, (1, LANES), 1)
+        for v in range(2):
+            low = nt_dot(vec, land_b[0, v])[0:1, EDGE - 1 : EDGE]
+            state[v : v + 1, 0:LANES] = jnp.where(
+                lane == LANES - 1, land_r[0, v : v + 1, :] + low, 0.0
+            )
+            high = nt_dot(vec, land_b[1, v])[0:1, 0:1]
+            state[v : v + 1, LANES + cells : 2 * LANES + cells] = jnp.where(
+                lane == 0, land_r[1, v : v + 1, :] + high, 0.0
+            )
+
+
+def halo(n, coords_now, coords_before, basis, ref):
+    cells, modes = basis.shape[1:]
+
+    def whole(shape):
+        return pl.BlockSpec(shape, lambda i: (0,) * len(shape))
+
+    wide = (8, cells + 2 * LANES)
+    edge = (2, 2, EDGE, modes)
     return pl.pallas_call(
         functools.partial(halo_kernel, n),
+        grid=(cells // TILE,),
         out_shape=[
-            jax.ShapeDtypeStruct((2, 2, EDGE, modes), jnp.bfloat16),
-            jax.ShapeDtypeStruct((2, 2, LANES), jnp.float32),
-        ],
-        in_specs=[pl.BlockSpec(memory_space=pl.ANY)] * 2,
-        out_specs=[vmem] * 2,
-        scratch_shapes=[pltpu.SemaphoreType.DMA((4,)), pltpu.SemaphoreType.DMA((4,))],
-        compiler_params=pltpu.CompilerParams(collective_id=0, has_side_effects=True),
-    )(basis, ref)
+            jax.ShapeDtypeStruct(edge, jnp.bfloat16),
+            jax.ShapeDtypeStruct(wide, jnp.float32),
+        ],
+        in_specs=[
+            whole(coords_now.shape),
+            whole(coords_before.shape),
+            whole(ref.shape),
+            pl.BlockSpec((2, TILE, modes), lambda i: (0, i, 0)),
+            pl.BlockSpec(memory_space=pl.ANY),
+            pl.BlockSpec(memory_space=pl.ANY),
+        ],
+        out_specs=[whole(edge), whole(wide)],
+        scratch_shapes=[
+            pltpu.VMEM(edge, jnp.bfloat16),
+            pltpu.VMEM((2, 2, LANES), jnp.float32),
+            pltpu.SemaphoreType.DMA((4,)),
+            pltpu.SemaphoreType.DMA((4,)),
+        ],
+        compiler_params=pltpu.CompilerParams(
+            collective_id=0, has_side_effects=True, vmem_limit_bytes=32 * 2**20
+        ),
+    )(coords_now, coords_before, ref, basis, basis, ref)
 
 
 def main_kernel(
-    stages, diffusivity, advection, rate, now_ref, before_ref, ref_ref, burn_ref, basis, before_rows,
-    after_rows, edge_b, edge_r,
+    stages, diffusivity, advection, rate, burn_ref, basis, before_rows, after_rows, edge_b, state,
     jac, res_out, packed,
-    state, coef, resid, wide, top, bottom, right,
+    coef, resid, wide, top, bottom, right,
 ):
-    phase, tile = pl.program_id(0), pl.program_id(1)
-    tiles = pl.num_programs(1)
+    tile, tiles = pl.program_id(0), pl.num_programs(0)
     cells = res_out.shape[1]
     modes = basis.shape[2]
     half = modes // 2
     here = pl.ds(pl.multiple_of(tile * TILE, TILE), TILE)
-    inner = pl.ds(pl.multiple_of(tile * TILE + LANES, LANES), TILE)
     h = time_step
     nu, c, k = diffusivity[0], advection[0], rate[0]
 
-    def coords():
-        now, old = now_ref[...], before_ref[...]
-        row = lax.broadcasted_iota(jnp.int32, (16, modes), 0)
-        both = jnp.where(row == 0, now, jnp.where(row == 1, now - old, 0.0))
-        return both.astype(jnp.bfloat16)
-
-    @pl.when(phase == 0)
-    def _():
-        vec = coords()
-
-        @pl.when(tile == 0)
-        def _():
-            state[...] = jnp.zeros_like(state)
-            resid[...] = jnp.zeros_like(resid)
-            lane = lax.broadcasted_iota(jnp.int32, (1, LANES), 1)
-            for v in range(2):
-                low = nt_dot(vec, edge_b[0, v])[0:1, EDGE - 1 : EDGE]
-                state[v : v + 1, 0:LANES] = jnp.where(
-                    lane == LANES - 1, edge_r[0, v : v + 1, :] + low, 0.0
-                )
-                high = nt_dot(vec, edge_b[1, v])[0:1, 0:1]
-                state[v : v + 1, LANES + cells : 2 * LANES + cells] = jnp.where(
-                    lane == 0, edge_r[1, v : v + 1, :] + high, 0.0
-                )
-
-        for v in range(2):
-            both = nt_dot(vec, basis[v])
-            state[v : v + 1, inner] = both[0:1] + ref_ref[v : v + 1, here]
-            state[v + 2 : v + 3, inner] = both[1:2]
-
-    @pl.when((phase == 1) & (tile == 0))
-    def _():
+    @pl.when(tile == 0)
+    def _():
+        resid[...] = jnp.zeros_like(resid)
         top[...] = jnp.zeros_like(top)
         bottom[...] = jnp.zeros_like(bottom)
         right[...] = jnp.zeros_like(right)
@@ -189,43 +208,41 @@
             span = slice(part * LANES, (part + 1) * LANES)
             coef[span, :] = stacked[:, span].T
 
-    @pl.when(phase == 1)
-    def _():
+    for v in range(2):
+        wide[v, 8 : 8 + TILE, :] = basis[v].astype(jnp.float32)
+        before = jnp.where(tile == 0, edge_b[0, v], before_rows[v]).astype(jnp.float32)
+        wide[v, 0:8, :] = before[EDGE - 8 : EDGE]
+        after = jnp.where(tile == tiles - 1, edge_b[1, v], after_rows[v]).astype(jnp.float32)
+        wide[v, 8 + TILE : 16 + TILE, :] = after[0:8]
+    base = 1.0 + 2.0 * h * nu + h * c
+    to_left = -h * (nu + c)
+    to_right = -h * nu
+
+    for start in range(0, TILE, ROWS):
+        at = pl.ds(pl.multiple_of(tile * TILE + start, ROWS), ROWS)
+        pair = coef[at, :]
+        ha, he = pair[:, 0:1], pair[:, 1:2]
+        centre, side = [], []
         for v in range(2):
-            wide[v, 8 : 8 + TILE, :] = basis[v].astype(jnp.float32)
-            before = jnp.where(tile == 0, edge_b[0, v], before_rows[v]).astype(jnp.float32)
-            wide[v, 0:8, :] = before[EDGE - 8 : EDGE]
-            after = jnp.where(tile == tiles - 1, edge_b[1, v], after_rows[v]).astype(jnp.float32)
-            wide[v, 8 + TILE : 16 + TILE, :] = after[0:8]
-        base = 1.0 + 2.0 * h * nu + h * c
-        to_left = -h * (nu + c)
-        to_right = -h * nu
-
-        for start in range(0, TILE, ROWS):
-            at = pl.ds(pl.multiple_of(tile * TILE + start, ROWS), ROWS)
-            pair = coef[at, :]
-            ha, he = pair[:, 0:1], pair[:, 1:2]
-            centre, side = [], []
-            for v in range(2):
-                centre.append(wide[v, 8 + start : 8 + start + ROWS, :])
-                side.append(
-                    to_left * wide[v, 7 + start : 7 + start + ROWS, :]
-                    + to_right * wide[v, 9 + start : 9 + start + ROWS, :]
-                )
-            fuel_rows = (base + ha) * centre[0] + side[0] + he * centre[1]
-            heat_rows = (base - he) * centre[1] + side[1] - ha * centre[0]
-            jac[0, start : start + ROWS, :] = fuel_rows.astype(jnp.bfloat16)
-            jac[1, start : start + ROWS, :] = heat_rows.astype(jnp.bfloat16)
-
-        rows = jac[...].reshape(2 * TILE, modes)
-        top[...] += tn_dot(rows[:, 0:half], rows)
-        bottom[...] += tn_dot(rows[:, half:], rows[:, half:])
-        both = resid[:, here].astype(jnp.bfloat16)
-        part_fuel = jnp.dot(both, jac[0], preferred_element_type=jnp.float32)
-        part_heat = jnp.dot(both, jac[1], preferred_element_type=jnp.float32)
-        right[...] += part_fuel[0:1] + part_heat[1:2]
-
-    @pl.when((phase == 1) & (tile == tiles - 1))
+            centre.append(wide[v, 8 + start : 8 + start + ROWS, :])
+            side.append(
+                to_left * wide[v, 7 + start : 7 + start + ROWS, :]
+                + to_right * wide[v, 9 + start : 9 + start + ROWS, :]
+            )
+        fuel_rows = (base + ha) * centre[0] + side[0] + he * centre[1]
+        heat_rows = (base - he) * centre[1] + side[1] - ha * centre[0]
+        jac[0, start : start + ROWS, :] = fuel_rows.astype(jnp.bfloat16)
+        jac[1, start : start + ROWS, :] = heat_rows.astype(jnp.bfloat16)
+
+    rows = jac[...].reshape(2 * TILE, modes)
+    top[...] += tn_dot(rows[:, 0:half], rows)
+    bottom[...] += tn_dot(rows[:, half:], rows[:, half:])
+    both = resid[:, here].astype(jnp.bfloat16)
+    part_fuel = jnp.dot(both, jac[0], preferred_element_type=jnp.float32)
+    part_heat = jnp.dot(both, jac[1], preferred_element_type=jnp.float32)
+    right[...] += part_fuel[0:1] + part_heat[1:2]
+
+    @pl.when(tile == tiles - 1)
     def _():
         packed[...] = jnp.zeros_like(packed)
         for stage, (offset, _) in enumerate(stages):
@@ -242,7 +259,7 @@
             packed[used + i : used + i + 1, :] = right[:, i * LANES : (i + 1) * LANES]
 
 
-def assemble(stages, packed_rows, params, coords_now, coords_before, ref, burning, basis, edges):
+def assemble(stages, packed_rows, params, burning, basis, edge_b, state):
     cells, modes = basis.shape[1:]
     tiles = cells // TILE
     per = TILE // EDGE
@@ -252,31 +269,30 @@
     half = modes // 2
 
     def whole(array):
-        return pl.BlockSpec(array.shape, lambda p, i: (0,) * array.ndim)
+        return pl.BlockSpec(array.shape, lambda i: (0,) * array.ndim)
 
     return pl.pallas_call(
         functools.partial(main_kernel, stages),
-        grid=(2, tiles),
+        grid=(tiles,),
         out_shape=[
             jax.ShapeDtypeStruct((2, cells, modes), jnp.bfloat16),
             jax.ShapeDtypeStruct((2, cells), jnp.float32),
             jax.ShapeDtypeStruct((packed_rows, LANES), jnp.float32),
         ],
         in_specs=[smem] * 3
-        + [whole(coords_now), whole(coords_before), whole(ref), whole(burning)]
+        + [whole(burning)]
         + [
-            pl.BlockSpec((2, TILE, modes), lambda p, i: (0, i, 0)),
-            pl.BlockSpec((2, EDGE, modes), lambda p, i: (0, jnp.maximum(i * per - 1, 0), 0)),
-            pl.BlockSpec((2, EDGE, modes), lambda p, i: (0, jnp.minimum((i + 1) * per, last), 0)),
+            pl.BlockSpec((2, TILE, modes), lambda i: (0, i, 0)),
+            pl.BlockSpec((2, EDGE, modes), lambda i: (0, jnp.maximum(i * per - 1, 0), 0)),
+            pl.BlockSpec((2, EDGE, modes), lambda i: (0, jnp.minimum((i + 1) * per, last), 0)),
         ]
-        + [whole(edge) for edge in edges],
+        + [whole(edge_b), whole(state)],
         out_specs=[
-            pl.BlockSpec((2, TILE, modes), lambda p, i: (0, i * p, 0)),
+            pl.BlockSpec((2, TILE, modes), lambda i: (0, i, 0)),
             vmem,
             vmem,
         ],
         scratch_shapes=[
-            pltpu.VMEM((8, cells + 2 * LANES), jnp.float32),
             pltpu.VMEM((cells, 8), jnp.float32),
             pltpu.VMEM((16, cells), jnp.float32),
             pltpu.VMEM((2, TILE + 16, modes), jnp.float32),
@@ -285,7 +301,7 @@
             pltpu.VMEM((1, modes), jnp.float32),
         ],
         compiler_params=pltpu.CompilerParams(vmem_limit_bytes=48 * 2**20),
-    )(*params, coords_now, coords_before, ref, burning, basis, basis, basis, *edges)
+    )(*params, burning, basis, basis, basis, edge_b, state)
 
 
 def layout(n, modes):
@@ -502,17 +518,15 @@
     n = lax.axis_size("space")
     modes = basis_rows.shape[2]
     stages, packed_rows = layout(n, modes)
-    edges = halo(n, basis_rows, reference_state)
+    edge_b, state = halo(n, coords_now, coords_before, basis_rows, reference_state)
     jacobian, residual, packed = assemble(
         stages,
         packed_rows,
         (diffusivity, advection, reaction_rate),
-        coords_now,
-        coords_before,
-        reference_state,
         burning[None],
         basis_rows,
-        edges,
+        edge_b,
+        state,
     )
     update = sum_and_solve(n, stages, modes, packed)
     return (jacobian[None], residual[None], update)

time: 88.3 us -> 85.4 us (0.967)
  Pallas kernels: 83.2 us -> 77 us
  local copies, waits for them, and re-layouts: 2.09 us -> 5.46 us
    pallas_call x2, Pallas kernels: 28.6 us -> 23.6 us  [the longest x1 14.4 us: assemble(): pl.pallas_call(functools.partial(main_kernel, stages), grid=(tiles,), out...]
    unnamed x13 -> x11, local copies, waits for them, and re-layouts: 2.09 us -> 5.46 us
    pallas_call x1, Pallas kernels: 54.6 us -> 53.4 us  [sum_and_solve(): pl.pallas_call(functools.partial(sum_solve_kernel, n, stages, modes), out...]
where the time goes in v3:
time: 85.4 us; the launch traced here: 85.1 us
  Pallas kernels  77 us (90%)
  local copies, waits for them, and re-layouts  5.46 us (6%)
  between operations  2.61 us (3%)
    pallas_call x1, Pallas kernels, sum_and_solve(): pl.pallas_call(functools.partial(sum_solve_kernel, n, stages, modes), out...  53.4 us
    pallas_call x1, Pallas kernels, assemble(): pl.pallas_call(functools.partial(main_kernel, stages), grid=(tiles,), out...  14.4 us
    pallas_call x1, Pallas kernels, halo(): pl.pallas_call(functools.partial(halo_kernel, n), grid=(cells // TILE,),...  9.26 us
    unnamed x11, local copies, waits for them, and re-layouts  5.46 us

profile of v3, /device:TPU:0, one launch (start us, length us, event | category | flops | bytes accessed | tf_op | source)
XLA Modules:
  0.0 85.1 jit_solution(10585186547160170197)
XLA Ops:
  2.6 0.0 copy-start
  2.6 2.8 %copy-done = bf16[2,3072,512]{2,1,0:T(8,128)(2,1)S(1)} copy-done((bf16[2,3072,512]{2,1,0:T(8,128)(2,1)S(1)}, bf16[2,3072,512]{2,1,0:T(8,128)(2,1)}, u32[]{:S(2)}) %copy-start) | copy-done | bytes 6291480
  5.4 0.0 copy-start.1
  5.4 0.7 copy-done.1
  6.1 0.0 copy-start.3
  6.1 0.7 copy-done.3
  6.8 0.0 copy-start.4
  6.8 0.7 copy-done.4
  7.5 0.0 copy-start.2
  7.5 9.3 %shard_map.103 = (bf16[2,2,16,512]{3,2,1,0:T(8,128)(2,1)S(1)}, f32[8,3328]{1,0:T(8,128)S(1)}) custom-call(f32[1,512]{1,0:T(1,128)S(1)} %copy-done.3, f32[1,512]{1,0:T(1,128)S(1)} %copy-done.4, f32[2,3072]{1,0:T(2,128)S(1)} %copy-done.1, bf16[2,3072,512]{2,1,0:T(8,128)(2,1)S(1)} %copy-done, bf16[2,3072,512]{2,1,0:T(8,128)(2,1)S(1)} %copy-done, ...), custom_call_target="tpu_custom_call" | custom-call | tf_op jit(solution)/shard_map/pallas_call | solution.py:140
  16.7 0.0 copy-done.2
  16.7 14.4 %shard_map.104 = (bf16[2,3072,512]{2,1,0:T(8,128)(2,1)}, f32[2,3072]{1,0:T(2,128)}, f32[1344,128]{1,0:T(8,128)S(1)}) custom-call(f32[1]{0:T(128)S(6)} %copy.12.diffusivity, f32[1]{0:T(128)S(6)} %copy.13.advection, f32[1]{0:T(128)S(6)} %copy.14.rate, s32[1,3072]{1,0:T(1,128)S(1)} %bitcast.3, bf16[2,3072,512]{2,1,0:T(8,128)(2,1)} %after_rows.1, ...), custom_call_target="tpu_custom_call" | custom-call | tf_op jit(solution)/shard_map/pallas_call | solution.py:274
  31.1 53.4 %shard_map.105 = f32[1,512]{1,0:T(1,128)S(1)} custom-call(f32[1344,128]{1,0:T(8,128)S(1)} %get-tuple-element.12.part), custom_call_target="tpu_custom_call" | custom-call | tf_op jit(solution)/shard_map/pallas_call | solution.py:484
  84.5 0.6 copy.15
Async XLA Ops:
  2.6 2.8 %copy-start = (bf16[2,3072,512]{2,1,0:T(8,128)(2,1)S(1)}, bf16[2,3072,512]{2,1,0:T(8,128)(2,1)}, u32[]{:S(2)}) copy-start(bf16[2,3072,512]{2,1,0:T(8,128)(2,1)} %after_rows.1) | copy-start | bytes 18874372
  5.4 0.7 copy-start.1
  6.1 0.7 copy-start.3
  6.8 0.7 copy-start.4
  7.5 9.3 %copy-start.2 = (s32[3072]{0:T(1024)S(1)}, s32[3072]{0:T(1024)}, u32[]{:S(2)}) copy-start(s32[3072]{0:T(1024)} %param.10) | copy-start | bytes 36868
